TPU v7x, 128 devices: a whole 4x4x4 slice. The times are simulated.
128 devices in a mesh: sec: 2 (over x_hi), oy: 8 (over z, core), ox: 8 (over x_lo, y).
Axes of the slice: x: 4 (x_hi: 2, x_lo: 2; x = x_hi * 2 + x_lo), y: 4, z: 4, core: 2. Of those that a mesh axis runs over, the one named last changes fastest.
Arguments:
- tracers: float32 [8, 62, 64, 2048], P('sec', None, 'oy', 'ox'), may hold values from -6 to 6
- zonal_velocity: float32 [62, 64, 2048], P(None, 'oy', 'ox'), may hold values from -0.12 to 0.12
- meridional_velocity: float32 [62, 64, 2048], P(None, 'oy', 'ox'), may hold values from -0.12 to 0.12
- diffusivity: float32 [62, 64, 2048], P(None, 'oy', 'ox'), may hold values from 0.01 to 0.12
- land_sea: int32 [64, 2048], P('oy', 'ox'), may hold values 0 or 1
- mix_class: int32 [64, 2048], P('oy', 'ox'), may hold values from 0 to 7
- mix_matrices: float32 [8, 62, 62], replicated, may hold values from 0 to 1
- atmos_fluxes: bfloat16 [8, 512, 1024], P(None, ('sec', 'oy'), 'ox'), may hold values from -6 to 6
- remap_weights: bfloat16 [8, 512, 4, 128, 128], P('ox', ('sec', 'oy')), may hold values from -0.1875 to 0.1875
- dest_tiles: int32 [8, 512, 4], replicated, may hold values from 0 to 127, all different within a row; in each aligned block of 32 rows (0 to 31, 32 to 63, ..., all dimensions but the last counted through in order) at most 2 rows name the same one
- dest_offsets: int32 [8, 512, 4], replicated, may hold values from 0 to 7
Outputs:
- new_tracers: float32 [8, 62, 64, 2048], P('sec', None, 'oy', 'ox')
- surface_flux: float32 [8, 64, 2048], P(None, 'oy', 'ox')
Inputs may be any that keep to these rules, and one draw needn't show every extreme that they name: `dest_tiles`: each atmosphere block names 4 different devices; among the rows of one device no device is named by more than 2 blocks, and some device by exactly 2.
All inputs are finite; a program needn't handle non-finite values. No bound on the sum of `land_sea` on one device may be relied on, other than what follows from the above.
Results may differ from a plain program's by a relative error of at most 0.0003.
Values sent between devices are 32-bit elements; how exact they have to be, the bound alone decides.
No kernel may reach another device: no remote copies, remote signals or barrier semaphores. Data moves between devices by JAX's collectives and lax.ppermute only.
A program may use at most 128 MiB of HBM per device.

v0:
```python
import jax
import jax.numpy as jnp
from jax import lax
from jax.experimental import pallas as pl
from jax.experimental.pallas import tpu as pltpu
from jax.sharding import PartitionSpec as P

F32 = jnp.float32
BF16 = jnp.bfloat16
MIB = 1024 * 1024
VM = pl.BlockSpec(memory_space=pltpu.VMEM)
SM = pl.BlockSpec(memory_space=pltpu.SMEM)
HB = pl.BlockSpec(memory_space=pltpu.HBM)
OY, OX, SEC, N_OY = 0, 1, 2, 3
UNROLL_ONE = 4
UNROLL_TWO = True
UNROLL_MIX = 4


def call(body, outs, in_specs, scratch=(), out_specs=None, limit=4):
    return pl.pallas_call(
        body,
        out_shape=outs,
        in_specs=in_specs,
        out_specs=out_specs or jax.tree.map(lambda _: VM, outs),
        scratch_shapes=list(scratch),
        compiler_params=pltpu.CompilerParams(vmem_limit_bytes=limit * MIB),
    )


def shape(*dims, dtype=F32):
    return jax.ShapeDtypeStruct(dims, dtype)


def to_tiles(x):
    lats, lons = x.shape[-2:]
    x = x.reshape(-1, lats, 2, lons // 2).transpose(0, 2, 1, 3)
    return x.reshape(-1, lons // 2)


def from_tiles(x, dims):
    x = x.reshape(-1, 2, dims[-2], x.shape[1]).transpose(0, 2, 1, 3)
    return x.reshape(dims)


def tile(ref, n):
    at = pl.multiple_of(n * 16, 16)
    return ref[pl.ds(at, 8), :], ref[pl.ds(at + 8, 8), :]


def put(ref, n, value):
    at = pl.multiple_of(n * 16, 16)
    ref[pl.ds(at, 8), :] = value[0]
    ref[pl.ds(at + 8, 8), :] = value[1]


def latitude(ref, row, count, first=0):
    return tuple(ref[pl.ds(first * 16 + h * 8 + row, count, stride=16), :] for h in range(2))


def one_row(ref, n):
    return ref[0, pl.ds(n, 1), :], ref[1, pl.ds(n, 1), :]


def fetch(pairs, sems):
    copies = [pltpu.make_async_copy(src, dst, sems.at[n]) for n, (src, dst) in enumerate(pairs)]
    for copy in copies:
        copy.start()
    return copies


def field_scratch(tr, u):
    return [pltpu.VMEM(tr.shape, F32)] + [pltpu.VMEM(u.shape, F32)] * 3 + [
        pltpu.VMEM((16, 128), jnp.int32), pltpu.SemaphoreType.DMA((12,))
    ]


def in_place(x):
    return pltpu.with_memory_space_constraint(x, pltpu.HBM)


def fetch_fields(hbm, vmem, sems):
    tr_hbm, tr_ref = hbm[0], vmem[0]
    rows = vmem[1].shape[0]
    cut = rows // 32 * 16
    parts = [
        pl.ds(at + first, size)
        for first, size in ((0, cut), (cut, rows - cut))
        for at in range(0, tr_ref.shape[0], rows)
    ]
    return fetch(
        list(zip(hbm[1:], vmem[1:])) + [(tr_hbm.at[part], tr_ref.at[part]) for part in parts], sems
    )


def remap_kernel(slot_ref, flux_ref, weight_hbm, out_ref, rows_ref, weight_ref, sems):
    fluxes, atm_rows, cells = flux_ref.shape
    dests = weight_ref.shape[1]
    chunks = sems.shape[0]
    size = atm_rows // chunks
    pieces = [pl.ds(n * size, size) for n in range(chunks)]
    copies = fetch([(weight_hbm.at[piece], weight_ref.at[piece]) for piece in pieces], sems)
    rows_ref[...] = flux_ref[...].astype(F32).reshape(fluxes * atm_rows, cells)
    out_ref[...] = jnp.zeros_like(out_ref)
    nothing = jnp.zeros((fluxes, cells), F32)
    for row in range(0, atm_rows, 2):
        if row % size == 0:
            copies[row // size].wait()
        one, two = (rows_ref[pl.ds(r, fluxes, stride=atm_rows), :] for r in (row, row + 1))
        lhs = jnp.concatenate(
            [jnp.concatenate([one, nothing], axis=1), jnp.concatenate([nothing, two], axis=1)], axis=0
        ).astype(BF16)
        for j in range(0, dests, 2):
            rhs = jnp.concatenate(
                [
                    jnp.concatenate([weight_ref[r, j], weight_ref[r, j + 1]], axis=1)
                    for r in (row, row + 1)
                ],
                axis=0,
            )
            parts = jnp.dot(lhs, rhs, preferred_element_type=F32)
            for r in range(2):
                for c in range(2):
                    out_ref[slot_ref[j + c, row + r]] = parts[r * fluxes : r * fluxes + fluxes, c * 128 : c * 128 + 128]


def table_kernel(sc_ref, dest_ref, offset_ref, out_ref):
    lons, dests, _ = dest_ref.shape
    lats = sc_ref[N_OY]
    pool = sc_ref[OY] * lons + sc_ref[OX]
    pools = out_ref.shape[1] // 4
    rows = lons * dests
    low = sc_ref[SEC] == 0
    dest = jnp.concatenate([dest_ref[q] for q in range(lons)], axis=0)
    offset = jnp.concatenate([offset_ref[q] for q in range(lons)], axis=0)
    width = dest.shape[1] // 2
    dest = jnp.where(low, dest[:, :width], dest[:, width:])
    offset = jnp.where(low, offset[:, :width], offset[:, width:])
    group = width // (pools // lons)

    def iota(dims, dim):
        return lax.broadcasted_iota(jnp.int32, dims, dim)

    def flag(x):
        return jnp.where(x, 1.0, 0.0).astype(BF16)

    square = (width, width)
    before = flag(
        (iota(square, 0) // group == iota(square, 1) // group) & (iota(square, 0) < iota(square, 1))
    )
    same_lon = flag(iota((rows, rows), 0) // dests == iota((rows, rows), 1) // dests)
    gather = (width, 128)
    spread = iota(gather, 0) // group == (iota(gather, 1) % pools) // lons
    spread = [flag(spread & (iota(gather, 1) // pools == r)) for r in range(2)]
    keep = iota((rows, 128), 0) // dests == iota((rows, 128), 1) % lons
    for s in range(2):
        hit = dest == pool + s * pools
        rank = jnp.dot(flag(hit), before, preferred_element_type=F32)
        rank = jnp.dot(same_lon, rank.astype(BF16), preferred_element_type=F32)
        place = ((offset & 1) * 8 + s * 4 + (offset >> 1) + 1).astype(F32)
        found = sum(
            jnp.dot(
                jnp.where(hit & (rank == float(r)), place, 0.0).astype(BF16), spread[r],
                preferred_element_type=F32,
            )
            for r in range(2)
        )
        found = jnp.sum(jnp.where(keep, found, 0.0), axis=0, keepdims=True)
        wanted = (iota((16, 128), 0) + 1).astype(F32)
        out_ref[:, s * 128 : s * 128 + 128] = jnp.where(found == wanted, 1.0, 0.0)


def combine_kernel(onehot_ref, recv_ref, after_ref, out_ref):
    fluxes = out_ref.shape[0] // 16
    slots = onehot_ref.shape[1]
    sources = slots // 4
    onehot = onehot_ref[...].astype(BF16)
    for f in range(fluxes):
        cells = jnp.concatenate(
            [recv_ref[pl.ds(n * fluxes + f, sources, stride=4 * fluxes), :] for n in range(4)],
            axis=0,
        )
        high = cells.astype(BF16)
        rest = cells - high.astype(F32)
        mid = rest.astype(BF16)
        low = (rest - mid.astype(F32)).astype(BF16)
        both = jnp.dot(
            onehot, jnp.concatenate([high, mid], axis=1), preferred_element_type=F32
        )
        out_ref[f * 16 : f * 16 + 16, :] = both[:, :128] + (
            both[:, 128:] + jnp.dot(onehot, low, preferred_element_type=F32)
        )


def pack_columns(fields, levels):
    lane = lax.broadcasted_iota(jnp.int32, (8, 128), 1)
    accs = [jnp.zeros((8, 128), F32) for _ in fields]
    for level in range(levels):
        west, east = lane == 2 * level, lane == 2 * level + 1
        for n, (ref, base) in enumerate(fields):
            first, last = tile(ref, base + level)
            acc = jnp.where(west, pltpu.roll(first, 2 * level, 1), accs[n])
            accs[n] = jnp.where(east, pltpu.roll(last, (2 * level + 2) % 128, 1), acc)
    return accs


def select_pair(even, x, y):
    return tuple(jnp.where(even, a, b) for a, b in zip(x, y))


def send_rows(even, north, south, ref_a, ref_b, at, count):
    for h in range(2):
        ref_a[h, at : at + count, :] = jnp.where(even, north[h], south[h])
        ref_b[h, at : at + count, :] = jnp.where(even, south[h], north[h])


def own_slots(sc_ref, dest_hbm, own_ref, sem):
    lons, dests, _ = dest_hbm.shape
    lats = sc_ref[N_OY]
    group = 32
    at = (sc_ref[SEC] * lats + sc_ref[OY]) * group
    aligned = pl.multiple_of(at // 128 * 128, 128)
    copy = pltpu.make_async_copy(dest_hbm.at[sc_ref[OX], :, pl.ds(aligned, 128)], own_ref, sem)
    copy.start()
    copy.wait()
    own = own_ref[...]
    own = jnp.concatenate([own, own], axis=0)
    own = pltpu.roll(own, (128 - (at - aligned)) % 128, 1)
    lane = lax.broadcasted_iota(jnp.int32, own.shape, 1)
    others = [own if n == 0 else pltpu.roll(own, n, 0) for n in range(dests)]
    again = jnp.zeros(own.shape, jnp.int32)
    for back in range(1, group):
        for other in others:
            again = jnp.where((own == pltpu.roll(other, back, 1)) & (lane >= back), 1, again)
    pools = lats * lons
    upper = jnp.where(own >= pools, 1, 0)
    return ((own - upper * pools) * 4 + upper * 2 + again)[:dests]


def pack_kernel(
    sc_ref, tr_hbm, u_hbm, v_hbm, k_hbm, land_hbm, dest_hbm, nsa_ref, nsb_ref, ew_ref, slot_ref,
    tr_ref, u_ref, v_ref, k_ref, land_ref, sems, own_ref, own_sem,
):
    copies = fetch_fields(
        (tr_hbm, u_hbm, v_hbm, k_hbm, land_hbm), (tr_ref, u_ref, v_ref, k_ref, land_ref), sems
    )
    levels = u_ref.shape[0] // 16
    tracers = tr_ref.shape[0] // u_ref.shape[0]
    count = tracers * levels
    even_y = sc_ref[OY] % 2 == 0
    v_at, k_at, w_at = count, count + 64, count + 128
    slot_ref[...] = own_slots(sc_ref, dest_hbm, own_ref, own_sem)
    for copy in copies[:4]:
        copy.wait()
    wet = tuple(x.astype(F32) for x in tile(land_ref, 0))
    for ref, n, at in ((v_ref, levels, v_at), (k_ref, levels, k_at)):
        send_rows(even_y, latitude(ref, 7, n), latitude(ref, 0, n), nsa_ref, nsb_ref, at, n)
    north = tuple(jnp.broadcast_to(x[7:8], x.shape) for x in wet)
    south = tuple(jnp.broadcast_to(x[0:1], x.shape) for x in wet)
    send_rows(even_y, north, south, nsa_ref, nsb_ref, w_at, 8)
    nothing = (jnp.zeros((64 - levels, 128), F32),) * 2
    for at in (v_at + levels, k_at + levels):
        send_rows(even_y, nothing, nothing, nsa_ref, nsb_ref, at, 64 - levels)

    for n, x in enumerate(pack_columns([(u_ref, 0), (k_ref, 0)], levels)):
        ew_ref[(tracers + n) * 8 : (tracers + n) * 8 + 8, :] = x
    for copy in copies[4:]:
        copy.wait()
    send_rows(even_y, latitude(tr_ref, 7, count), latitude(tr_ref, 0, count), nsa_ref, nsb_ref, 0, count)
    for n, x in enumerate(pack_columns([(tr_ref, t * levels) for t in range(tracers)], levels)):
        ew_ref[n * 8 : n * 8 + 8, :] = x
    odd = lax.broadcasted_iota(jnp.int32, (8, 128), 1) % 2 == 1
    ew_ref[(tracers + 2) * 8 :, :] = jnp.where(odd, wet[1][:, 127:], wet[0][:, :1])


def east_of(x, rim):
    lane = lax.broadcasted_iota(jnp.int32, (8, 128), 1)
    first, last = (pltpu.roll(half, 127, 1) for half in x)
    return jnp.where(lane == 127, last, first), jnp.where(lane == 127, rim, last)


def west_of(x, rim):
    lane = lax.broadcasted_iota(jnp.int32, (8, 128), 1)
    first, last = (pltpu.roll(half, 1, 1) for half in x)
    return jnp.where(lane == 0, rim, first), jnp.where(lane == 0, first, last)


def north_of(x, rim):
    row = lax.broadcasted_iota(jnp.int32, (8, 128), 0)
    return tuple(jnp.where(row == 7, r, pltpu.roll(half, 7, 0)) for half, r in zip(x, rim))


def south_of(x, rim):
    row = lax.broadcasted_iota(jnp.int32, (8, 128), 0)
    return tuple(jnp.where(row == 0, r, pltpu.roll(half, 1, 0)) for half, r in zip(x, rim))


def to_ends(rim, level):
    return pltpu.roll(rim, 127 - 2 * level, 1)


def face(vel_left, vel_right, dif_left, dif_right, ww):
    velocity = 0.5 * (vel_left + vel_right)
    spread = 0.5 * (dif_left + dif_right)
    return (
        ww * (jnp.maximum(velocity, 0.0) + spread),
        ww * (jnp.minimum(velocity, 0.0) - spread),
    )


def stencil(coefs, x, rim, north, south):
    middle, ce, cw, cn, cs = coefs
    e, w, n, s = east_of(x, rim), west_of(x, rim), north_of(x, north), south_of(x, south)
    return tuple(
        (middle[h] * x[h] + (ce[h] * e[h] + cw[h] * w[h])) + (cn[h] * n[h] + cs[h] * s[h])
        for h in range(2)
    )


def merge_columns(sc_ref, ewa_ref, ewb_ref):
    even = sc_ref[OX] % 2 == 0
    a, b = ewa_ref[...], ewb_ref[...]
    first = lax.broadcasted_iota(jnp.int32, a.shape, 1) % 2 == 0
    return jnp.where(first, jnp.where(even, a, b), jnp.where(even, b, a))


def merge_rows(sc_ref, nsa_ref, nsb_ref, north_ref, south_ref):
    even = sc_ref[OY] % 2 == 0
    for h in range(2):
        a, b = nsa_ref[h], nsb_ref[h]
        north_ref[h] = jnp.where(even, a, b)
        south_ref[h] = jnp.where(even, b, a)


def step_one_kernel(
    sc_ref, tr_hbm, u_hbm, v_hbm, k_hbm, land_hbm, nsa_hbm, nsb_hbm, ewa_hbm, ewb_hbm, own_hbm,
    new_hbm, coef_hbm, nsa_out, nsb_out, ew_out,
    north_ref, south_ref, face_ref, tr_ref, u_ref, v_ref, k_ref, land_ref, sems,
    nsa_ref, nsb_ref, ewa_ref, ewb_ref, own_ref, rim_sems, new_ref, coef_ref, out_sems,
):
    rim_copies = fetch(
        (
            (nsa_hbm, nsa_ref), (nsb_hbm, nsb_ref), (ewa_hbm, ewa_ref), (ewb_hbm, ewb_ref),
            (own_hbm, own_ref),
        ),
        rim_sems,
    )
    copies = fetch_fields(
        (tr_hbm, u_hbm, v_hbm, k_hbm, land_hbm), (tr_ref, u_ref, v_ref, k_ref, land_ref), sems
    )
    levels = u_ref.shape[0] // 16
    tracers = tr_ref.shape[0] // u_ref.shape[0]
    count = tracers * levels
    even_y = sc_ref[OY] % 2 == 0
    keep_north = (sc_ref[OY] < sc_ref[N_OY] - 1).astype(F32)
    keep_south = (sc_ref[OY] > 0).astype(F32)
    v_at, k_at, w_at = count, count + 64, count + 128
    for copy in rim_copies:
        copy.wait()
    merge_rows(sc_ref, nsa_ref, nsb_ref, north_ref, south_ref)
    for copy in copies[:4]:
        copy.wait()
    wet = tuple(x.astype(F32) for x in tile(land_ref, 0))
    for side, (ref, row, keep) in enumerate(((north_ref, 7, keep_north), (south_ref, 0, keep_south))):
        v_own, k_own = latitude(v_ref, row, levels), latitude(k_ref, row, levels)
        for h in range(2):
            pieces = face(
                v_own[h], ref[h, v_at : v_at + levels, :], k_own[h], ref[h, k_at : k_at + levels, :],
                wet[h][row : row + 1] * ref[h, w_at : w_at + 1, :] * keep,
            )
            for n, x in enumerate(pieces):
                face_ref[side * 2 + n, h, :levels, :] = x
    rims = merge_columns(sc_ref, ewa_ref, ewb_ref)
    own = own_ref[8 * tracers :, :]
    first = lax.broadcasted_iota(jnp.int32, own.shape, 1) % 2 == 0
    own = jnp.where(first, pltpu.roll(own, 127, 1), pltpu.roll(own, 1, 1))
    rim_u, rim_k, rim_w = (rims[8 * (tracers + n) : 8 * (tracers + n + 1)] for n in range(3))
    side_a, side_b = face(own[:8], rim_u, own[8:16], rim_k, own[16:] * rim_w)

    nothing = jnp.zeros((8, 128), F32)
    ww_east = tuple(w * e for w, e in zip(wet, east_of(wet, nothing)))
    ww_north = tuple(w * n for w, n in zip(wet, north_of(wet, (nothing, nothing))))
    last_lane = lax.broadcasted_iota(jnp.int32, (8, 128), 1) == 127
    top_row = lax.broadcasted_iota(jnp.int32, (8, 128), 0) == 7

    def body(level, _):
        ul, vl, kl = tile(u_ref, level), tile(v_ref, level), tile(k_ref, level)
        ue, ke = east_of(ul, nothing), east_of(kl, nothing)
        vn = tuple(pltpu.roll(half, 7, 0) for half in vl)
        kn = tuple(pltpu.roll(half, 7, 0) for half in kl)
        ae, be = zip(*(face(ul[h], ue[h], kl[h], ke[h], ww_east[h]) for h in range(2)))
        an, bn = zip(*(face(vl[h], vn[h], kl[h], kn[h], ww_north[h]) for h in range(2)))
        ends_a, ends_b = to_ends(side_a, level), to_ends(side_b, level)
        ae = ae[0], jnp.where(last_lane, ends_a, ae[1])
        be = be[0], jnp.where(last_lane, ends_b, be[1])
        aw, bw = west_of(ae, ends_a), west_of(be, ends_b)
        an = tuple(jnp.where(top_row, r, x) for r, x in zip(one_row(face_ref.at[0], level), an))
        bn = tuple(jnp.where(top_row, r, x) for r, x in zip(one_row(face_ref.at[1], level), bn))
        as_ = south_of(an, one_row(face_ref.at[2], level))
        bs = south_of(bn, one_row(face_ref.at[3], level))
        middle = tuple(((1.0 - ae[h]) + bw[h]) + (bs[h] - an[h]) for h in range(2))
        coefs = middle, tuple(-x for x in be), aw, tuple(-x for x in bn), as_
        for n, x in enumerate(coefs):
            put(coef_ref, level * 5 + n, x)
        for t in range(tracers):
            n = t * levels + level
            put(
                new_ref, n,
                stencil(
                    coefs, tile(tr_ref, n), to_ends(rims[8 * t : 8 * t + 8], level),
                    one_row(north_ref, n), one_row(south_ref, n),
                ),
            )
        return 0

    out = []
    for n, first, last in ((0, 0, levels // 2), (1, levels // 2, levels)):
        for copy in copies[4 + n * tracers : 4 + n * tracers + tracers]:
            copy.wait()
        lax.fori_loop(first, last, body, 0, unroll=UNROLL_ONE)
        pieces = [(coef_ref, coef_hbm, first * 5, last * 5)]
        pieces += [(new_ref, new_hbm, t * levels + first, t * levels + last) for t in range(tracers)]
        for i, (src, dst, a, b) in enumerate(pieces):
            part = pl.ds(a * 16, (b - a) * 16)
            out.append(pltpu.make_async_copy(src.at[part], dst.at[part], out_sems.at[n * len(pieces) + i]))
            out[-1].start()
    for n, x in enumerate(pack_columns([(new_ref, t * levels) for t in range(tracers)], levels)):
        ew_out[n * 8 : n * 8 + 8, :] = x
    send_rows(
        even_y, latitude(new_ref, 7, count), latitude(new_ref, 0, count), nsa_out, nsb_out, 0, count
    )
    for copy in out:
        copy.wait()


def prepare_kernel(mats_ref, class_ref, lhs_ref, unit_ref, rows_ref):
    levels, classes, _ = mats_ref.shape
    rows_ref[:, :levels] = mats_ref[...].reshape(levels * classes, levels)
    lhs_ref[...] = jnp.zeros_like(lhs_ref)
    tops = []
    for k in range(classes):
        m = rows_ref[pl.ds(k, levels, stride=classes), :]
        high = m.astype(BF16)
        low = (m - high.astype(F32)).astype(BF16)
        for n, x in enumerate((high, low, high)):
            lhs_ref[k * 64 : k * 64 + levels, n * 64 : n * 64 + levels] = x[:, :levels]
        tops.append([jnp.broadcast_to(m[:, n : n + 1], (levels, 128)) for n in range(2)])
    for lat in range(8):
        for h in range(2):
            kind = class_ref[h * 8 + lat : h * 8 + lat + 1, :]
            for n in range(2):
                unit = tops[0][n]
                for k in range(1, classes):
                    unit = jnp.where(kind == k, tops[k][n], unit)
                unit_ref[pl.ds(n * levels * 16 + h * 8 + lat, levels, stride=16), :] = unit


def step_two_kernel(
    sc_ref, tr_hbm, coef_hbm, nsa_ref, nsb_ref, ewa_ref, ewb_ref, lhs_ref, class_ref,
    pre_ref, top_ref,
    north_ref, south_ref, cells_ref, tr_ref, coef_ref, sems,
):
    levels = coef_ref.shape[0] // 80
    tracers = tr_ref.shape[0] // (levels * 16)
    parts = (0, levels // 4), (levels // 4, levels)
    pieces = []
    for a, b in parts:
        pieces.append((coef_hbm, coef_ref, a * 5, b * 5))
        pieces += [(tr_hbm, tr_ref, t * levels + a, t * levels + b) for t in range(tracers)]
    copies = fetch(
        [(src.at[pl.ds(a * 16, (b - a) * 16)], dst.at[pl.ds(a * 16, (b - a) * 16)]) for src, dst, a, b in pieces],
        sems,
    )
    classes = lhs_ref.shape[0] // 64
    merge_rows(sc_ref, nsa_ref, nsb_ref, north_ref, south_ref)
    rims = merge_columns(sc_ref, ewa_ref, ewb_ref)

    def body(level, _):
        coefs = [tile(coef_ref, level * 5 + n) for n in range(5)]
        for t in range(tracers):
            n = t * levels + level
            put(
                cells_ref, t * 64 + level,
                stencil(
                    coefs, tile(tr_ref, n), to_ends(rims[8 * t : 8 * t + 8], level),
                    one_row(north_ref, n), one_row(south_ref, n),
                ),
            )
        return 0

    for n, (first, last) in enumerate(parts):
        for copy in copies[n * (tracers + 1) : (n + 1) * (tracers + 1)]:
            copy.wait()
        lax.fori_loop(first, last, body, 0, unroll=UNROLL_TWO)
    for t in range(tracers):
        at = t * 1024
        top_ref[t * 32 : t * 32 + 32, :] = cells_ref[at : at + 32, :]
        cells_ref[at : at + 32, :] = jnp.zeros((32, 128), F32)
        cells_ref[at + levels * 16 : at + 1024, :] = jnp.zeros((1024 - levels * 16, 128), F32)

    def mix(n, _):
        t, lat = n // 8, n % 8
        x = jnp.concatenate(
            [cells_ref[pl.ds(t * 1024 + h * 8 + lat, 64, stride=16), :] for h in range(2)], axis=1
        )
        high = x.astype(BF16)
        low = (x - high.astype(F32)).astype(BF16)
        mixed = jnp.dot(
            lhs_ref[...], jnp.concatenate([high, high, low], axis=0), preferred_element_type=F32
        )
        for h in range(2):
            lanes = slice(h * 128, h * 128 + 128)
            kind = class_ref[pl.ds(h * 8 + lat, 1), :]
            out = mixed[:64, lanes]
            for k in range(1, classes):
                out = jnp.where(kind == k, mixed[k * 64 : k * 64 + 64, lanes], out)
            pre_ref[pl.ds(t * levels * 16 + h * 8 + lat, levels, stride=16), :] = out[:levels]
        return 0

    lax.fori_loop(0, tracers * 8, mix, 0, unroll=UNROLL_MIX)


def finish_kernel(sc_ref, mine_ref, other_ref, land_ref, top_ref, unit_ref, pre_ref, out_ref, surface_ref):
    levels = unit_ref.shape[0] // 32
    tracers = pre_ref.shape[0] // (levels * 16)
    new = [[], []]
    for h in range(2):
        half = pl.ds(h * 8, 8)
        flux = [
            mine_ref[f * 16 + h * 8 : f * 16 + h * 8 + 8] + other_ref[f * 16 + h * 8 : f * 16 + h * 8 + 8]
            for f in range(8)
        ]
        for f in range(8):
            surface_ref[f * 16 + h * 8 : f * 16 + h * 8 + 8, :] = flux[f]
        wet = land_ref[half, :].astype(F32)
        heat = flux[0] + flux[1] + flux[2] + flux[3]
        fresh = flux[5] - flux[4]
        stress = 0.5 * (flux[6] * flux[6] + flux[7] * flux[7])
        weight = wet * 0.5 * stress / (1.0 + stress)
        for t in range(tracers):
            select = ((sc_ref[SEC] == 0) & (t == 0)).astype(F32)
            top = top_ref[t * 32 + h * 8 : t * 32 + h * 8 + 8, :]
            second = top_ref[t * 32 + 16 + h * 8 : t * 32 + 24 + h * 8, :]
            top = top + wet * (0.25 * select * heat + 0.1 * (1.0 - select) * fresh * top)
            new[h].append((top + weight * (second - top), second + weight * (top - second)))
    for level in range(levels):
        m0, m1 = tile(unit_ref, level), tile(unit_ref, levels + level)
        for t in range(tracers):
            x = tile(pre_ref, t * levels + level)
            put(
                out_ref, t * levels + level,
                tuple(x[h] + (m0[h] * new[h][t][0] + m1[h] * new[h][t][1]) for h in range(2)),
            )


def swap(x, axis, odd):
    n = lax.axis_size(axis)
    pairs = []
    for i in range(n // 2):
        left = (2 * i + odd) % n
        right = (left + 1) % n
        pairs += [(left, right), (right, left)]
    return lax.ppermute(x, axis, pairs)


def per_device(
    tracers, zonal_velocity, meridional_velocity, diffusivity, land_sea, mix_class, mix_matrices,
    atmos_fluxes, remap_weights, dest_tiles, dest_offsets,
):
    count, levels, lats, lons = tracers.shape
    n_oy, n_ox = lax.axis_size("oy"), lax.axis_size("ox")
    pools = n_oy * n_ox
    oy, ox, sec = lax.axis_index("oy"), lax.axis_index("ox"), lax.axis_index("sec")
    sc = jnp.stack([oy, ox, sec, jnp.int32(n_oy)]).astype(jnp.int32)
    fluxes, atm_rows, cells = atmos_fluxes.shape
    dests = dest_tiles.shape[2]
    classes = mix_matrices.shape[0]
    tr, u, v, k = (
        to_tiles(x) for x in (tracers, zonal_velocity, meridional_velocity, diffusivity)
    )
    land, kinds = to_tiles(land_sea), to_tiles(mix_class)

    tr, u, v, k, land_hbm, sc = (in_place(x) for x in (tr, u, v, k, land, sc))
    dest_t = dest_tiles.transpose(0, 2, 1)
    offset_t = dest_offsets.transpose(0, 2, 1)
    rows = count * levels + 136
    edge = 8 * (count + 3)
    nsa, nsb, ew, slots = call(
        pack_kernel,
        (shape(2, rows, 128), shape(2, rows, 128), shape(edge, 128), shape(dests, 128, dtype=jnp.int32)),
        [SM] + [HB] * 6,
        field_scratch(tr, u) + [pltpu.VMEM((dests, 128), jnp.int32), pltpu.SemaphoreType.DMA], limit=8,
    )(sc, tr, u, v, k, land_hbm, in_place(dest_t))
    nsa_in, nsb_in = swap(nsa, "oy", 0), swap(nsb, "oy", 1)
    ewa_in, ewb_in = swap(ew, "ox", 0), swap(ew, "ox", 1)

    blocks = call(
        remap_kernel,
        shape(pools * 4, fluxes, 128),
        [SM, VM, HB],
        [
            pltpu.VMEM((fluxes * atm_rows, cells), F32),
            pltpu.VMEM(remap_weights.shape[1:], BF16), pltpu.SemaphoreType.DMA((8,)),
        ],
        limit=8,
    )(slots, atmos_fluxes, in_place(remap_weights[0]))
    blocks, nsa_in, nsb_in, ewa_in, ewb_in = lax.optimization_barrier(
        (blocks, nsa_in, nsb_in, ewa_in, ewb_in)
    )
    routed = lax.all_to_all(
        blocks.reshape(pools, 4 * fluxes, 128), ("oy", "ox"), split_axis=0, concat_axis=0, tiled=True
    )

    onehot = call(table_kernel, shape(16, pools * 4), [SM, VM, VM])(sc, dest_t, offset_t)
    lhs, units = call(
        prepare_kernel,
        (shape(64 * classes, 192, dtype=BF16), shape(2 * levels * 16, 128)),
        [VM, VM],
        [pltpu.VMEM((levels * classes, 128), F32)],
    )(mix_matrices.transpose(1, 0, 2), kinds)

    moved, coef, nsa, nsb, ew = call(
        step_one_kernel,
        (
            shape(*tr.shape), shape(5 * levels * 16, 128),
            shape(2, count * levels, 128), shape(2, count * levels, 128), shape(8 * count, 128),
        ),
        [SM] + [HB] * 10,
        [pltpu.VMEM((2, rows, 128), F32), pltpu.VMEM((2, rows, 128), F32), pltpu.VMEM((4, 2, 64, 128), F32)]
        + field_scratch(tr, u)
        + [pltpu.VMEM((2, rows, 128), F32)] * 2
        + [pltpu.VMEM((edge, 128), F32)] * 3
        + [
            pltpu.SemaphoreType.DMA((5,)), pltpu.VMEM(tr.shape, F32),
            pltpu.VMEM((5 * levels * 16, 128), F32), pltpu.SemaphoreType.DMA((10,)),
        ],
        [HB, HB, VM, VM, VM],
        60,
    )(sc, tr, u, v, k, land_hbm, *(in_place(x) for x in (nsa_in, nsb_in, ewa_in, ewb_in, ew)))
    nsa_in, nsb_in = swap(nsa, "oy", 0), swap(nsb, "oy", 1)
    ewa_in, ewb_in = swap(ew, "ox", 0), swap(ew, "ox", 1)

    routed, ewa_in, ewb_in = lax.optimization_barrier((routed, ewa_in, ewb_in))
    mine = call(combine_kernel, shape(fluxes * 16, 128), [VM] * 3)(
        onehot, routed.reshape(pools * 4 * fluxes, 128), lhs
    )
    pre, top = call(
        step_two_kernel,
        (shape(*tr.shape), shape(32 * count, 128)),
        [SM, HB, HB] + [VM] * 6,
        [
            pltpu.VMEM((2, count * levels, 128), F32), pltpu.VMEM((2, count * levels, 128), F32),
            pltpu.VMEM((count * 1024, 128), F32), pltpu.VMEM(tr.shape, F32),
            pltpu.VMEM(coef.shape, F32), pltpu.SemaphoreType.DMA((10,)),
        ],
        limit=12,
    )(sc, in_place(moved), in_place(coef), nsa_in, nsb_in, ewa_in, ewb_in, lhs, kinds)

    other = swap(mine, "sec", 0)
    out, surface = call(
        finish_kernel, (shape(*tr.shape), shape(fluxes * 16, 128)), [SM] + [VM] * 6
    )(sc, mine, other, land, top, units, pre)
    return from_tiles(out, tracers.shape), from_tiles(surface, (fluxes, lats, lons))


def solution(mesh):
    placed = (
        P("sec", None, "oy", "ox"),
        P(None, "oy", "ox"),
        P(None, "oy", "ox"),
        P(None, "oy", "ox"),
        P("oy", "ox"),
        P("oy", "ox"),
        P(),
        P(None, ("sec", "oy"), "ox"),
        P("ox", ("sec", "oy"), None, None, None),
        P(),
        P(),
    )
    return jax.shard_map(
        per_device,
        mesh=mesh,
        in_specs=placed,
        out_specs=(P("sec", None, "oy", "ox"), P(None, "oy", "ox")),
        check_vma=False,
    )
```

profile of v0, /device:TPU:0, one launch (start us, length us, event | category | flops | bytes accessed | tf_op | source)
XLA Modules:
  0.0 59.1 jit_solution(17328391643335593025)
XLA Ops:
  0.6 0.7 %pad_add_fusion.sc_ref = s32[4]{0:T(128)} fusion(s32[1]{0:T(128)} %constant.14.clone.1, s32[1]{0:T(128)} %bitcast.2, s32[1]{0:T(128)} %bitcast.1, s32[1]{0:T(128)} %bitcast), kind=kLoop, calls=%fused_computation | loop fusion | flops 12 | bytes 32 | tf_op jit(solution)/shard_map/stack | solution.py:574
  1.3 4.0 %shard_map.123 = (f32[2,384,128]{2,1,0:T(8,128)S(1)}, f32[2,384,128]{2,1,0:T(8,128)S(1)}, f32[56,128]{1,0:T(8,128)S(1)}, s32[4,128]{1,0:T(4,128)S(1)}) custom-call(s32[4]{0:T(128)} %pad_add_fusion.sc_ref, f32[3968,128]{1,0:T(8,128)} %bitcast.59, f32[992,128]{1,0:T(8,128)} %bitcast.62, f32[992,128]{1,0:T(8,128)} %bitcast.64, f32[992,128]{1,0:T(8,128)} %bitcast.66, ...), custom_call_target="tpu_custom_call" | custom-call | tf_op jit(solution)/shard_map/pallas_call | solution.py:588
  5.3 0.1 collective-permute-start
  5.4 4.2 %collective-permute-start.1 = (f32[2,384,128]{2,1,0:T(8,128)S(1)}, f32[2,384,128]{2,1,0:T(8,128)S(1)}, u32[]{:S(2)}, u32[]{:S(2)}) collective-permute-start(f32[2,384,128]{2,1,0:T(8,128)S(1)} %get-tuple-element.27), channel_id=1, source_target_pairs={{8,16},{16,8},{24,32},{32,24},{40,48},{48,40},{56,0},{0,56},{9,17}... | collective-permute-start | bytes 1179656 | tf_op jit(solution)/shard_map/ppermute | solution.py:563
  9.6 3.9 %collective-permute-start.3 = (f32[56,128]{1,0:T(8,128)S(1)}, f32[56,128]{1,0:T(8,128)S(1)}, u32[]{:S(2)}, u32[]{:S(2)}) collective-permute-start(f32[56,128]{1,0:T(8,128)S(1)} %get-tuple-element.28.own_hbm), channel_id=1, source_target_pairs={{1,2},{2,1},{3,4},{4,3},{5,6},{6,5},{7,0},{0,7},{9,10},{10,9},{11,... | collective-permute-start | bytes 86024 | tf_op jit(solution)/shard_map/ppermute | solution.py:563
  13.6 0.0 collective-permute-start.2
  13.6 4.1 %shard_map.124 = f32[256,8,128]{2,1,0:T(8,128)} custom-call(s32[4,128]{1,0:T(4,128)S(1)} %get-tuple-element.25.slot_ref, bf16[8,32,128]{2,1,0:T(8,128)(2,1)S(1)} %copy-done.3, bf16[32,4,128,128]{3,2,1,0:T(8,128)(2,1)} %bitcast.61), custom_call_target="tpu_custom_call" | custom-call | tf_op jit(solution)/shard_map/pallas_call | solution.py:597
  17.7 0.0 collective-permute-done.3.ewb_hbm
  17.8 0.0 collective-permute-done.2.ewa_hbm
  17.8 0.0 copy-start.10
  17.8 0.0 collective-permute-done.nsa_hbm
  17.8 6.1 %all-to-all-start = ((f32[64,32,128]{2,1,0:T(8,128)}), f32[64,32,128]{2,1,0:T(8,128)S(1)}, u32[]{:S(2)}, u32[]{:S(2)}) async-start(f32[64,32,128]{2,1,0:T(8,128)} %bitcast.21), calls=%async_computation | async-start | bytes 2097152 | tf_op jit(solution)/shard_map/all_to_all | solution.py:610
  23.9 0.0 copy-start
  24.0 0.0 copy-start.4
  24.0 0.0 copy-start.1
  24.0 0.0 copy-start.5
  24.0 10.2 %shard_map.125 = (f32[3968,128]{1,0:T(8,128)}, f32[4960,128]{1,0:T(8,128)}, f32[2,248,128]{2,1,0:T(8,128)}, f32[2,248,128]{2,1,0:T(8,128)}, f32[32,128]{1,0:T(8,128)}) custom-call(s32[4]{0:T(128)} %pad_add_fusion.sc_ref, f32[3968,128]{1,0:T(8,128)} %bitcast.60, f32[992,128]{1,0:T(8,128)} %bitcast.63, f32[992,128]{1,0:T(8,128)} %bitcast.65, ...), custom_call_target="tpu_custom_call" | custom-call | tf_op jit(solution)/shard_map/pallas_call | solution.py:622
  34.2 0.1 collective-permute-start.7
  34.3 3.0 %collective-permute-start.8 = (f32[2,248,128]{2,1,0:T(8,128)}, f32[2,248,128]{2,1,0:T(8,128)S(1)}, u32[]{:S(2)}, u32[]{:S(2)}) collective-permute-start(f32[2,248,128]{2,1,0:T(8,128)} %get-tuple-element.40), channel_id=1, source_target_pairs={{8,16},{16,8},{24,32},{32,24},{40,48},{48,40},{56,0},{0,56},{9,17}... | collective-permute-start | bytes 761864 | tf_op jit(solution)/shard_map/ppermute | solution.py:563
  37.4 3.6 %collective-permute-start.5 = (f32[32,128]{1,0:T(8,128)}, f32[32,128]{1,0:T(8,128)S(1)}, u32[]{:S(2)}, u32[]{:S(2)}) collective-permute-start(f32[32,128]{1,0:T(8,128)} %get-tuple-element.34), channel_id=1, source_target_pairs={{1,2},{2,1},{3,4},{4,3},{5,6},{6,5},{7,0},{0,7},{9,10},{10,9},{11,... | collective-permute-start | bytes 49160 | tf_op jit(solution)/shard_map/ppermute | solution.py:563
  41.0 0.0 collective-permute-start.4
  41.0 1.2 %shard_map.122.onehot_ref = f32[16,256]{1,0:T(8,128)S(1)} custom-call(s32[4]{0:T(128)} %pad_add_fusion.sc_ref, s32[8,4,512]{2,1,0:T(4,128)S(1)} %bitcast.51, s32[8,4,512]{2,1,0:T(4,128)S(1)} %bitcast.56), custom_call_target="tpu_custom_call" | custom-call | tf_op jit(solution)/shard_map/pallas_call | solution.py:614
  42.3 0.8 %shard_map.126 = (bf16[512,192]{1,0:T(8,128)(2,1)S(1)}, f32[1984,128]{1,0:T(8,128)S(1)}) custom-call(f32[62,8,62]{2,1,0:T(8,128)S(1)} %bitcast.52, s32[16,128]{1,0:T(8,128)S(1)} %bitcast.57), custom_call_target="tpu_custom_call" | custom-call | tf_op jit(solution)/shard_map/pallas_call | solution.py:615
  43.1 0.3 collective-permute-done.5.ewb_ref
  43.4 1.5 %collective-permute-done.4.ewa_ref = f32[32,128]{1,0:T(8,128)S(1)} collective-permute-done((f32[32,128]{1,0:T(8,128)}, f32[32,128]{1,0:T(8,128)S(1)}, u32[]{:S(2)}, u32[]{:S(2)}) %collective-permute-start.4) | collective-permute-done | bytes 16416 | tf_op jit(solution)/shard_map/ppermute | solution.py:563
  44.9 0.0 all-to-all-done
  44.9 0.7 %shard_map.127.mine_ref = f32[128,128]{1,0:T(8,128)S(1)} custom-call(f32[16,256]{1,0:T(8,128)S(1)} %shard_map.122.onehot_ref, f32[2048,128]{1,0:T(8,128)S(1)} %bitcast.49, bf16[512,192]{1,0:T(8,128)(2,1)S(1)} %get-tuple-element.36.after_ref.lhs_ref), custom_call_target="tpu_custom_call" | custom-call | tf_op jit(solution)/shard_map/pallas_call | solution.py:644
  45.7 2.7 %collective-permute-start.6 = (f32[128,128]{1,0:T(8,128)S(1)}, f32[128,128]{1,0:T(8,128)S(1)}, u32[]{:S(2)}, u32[]{:S(2)}) collective-permute-start(f32[128,128]{1,0:T(8,128)S(1)} %shard_map.127.mine_ref), channel_id=1, source_target_pairs={{0,64},{64,0},{1,65},{65,1},{2,66},{66,2},{3,67},{67,3},{4,68},{68... | collective-permute-start | bytes 196616 | tf_op jit(solution)/shard_map/ppermute | solution.py:563
  48.4 0.0 collective-permute-done.7.nsa_ref
  48.4 0.0 collective-permute-done.8.nsb_ref
  48.4 8.4 %shard_map.128 = (f32[3968,128]{1,0:T(8,128)S(1)}, f32[128,128]{1,0:T(8,128)S(1)}) custom-call(s32[4]{0:T(128)} %pad_add_fusion.sc_ref, f32[3968,128]{1,0:T(8,128)} %get-tuple-element.37.tr_hbm, f32[4960,128]{1,0:T(8,128)} %get-tuple-element.38.coef_hbm, f32[2,248,128]{2,1,0:T(8,128)S(1)} %collective-permute-done.7.nsa_ref, ...), custom_call_target="tpu_custom_call" | custom-call | tf_op jit(solution)/shard_map/pallas_call | solution.py:647
  56.8 2.3 %shard_map.129 = (f32[3968,128]{1,0:T(8,128)}, f32[128,128]{1,0:T(8,128)}) custom-call(s32[4]{0:T(128)} %pad_add_fusion.sc_ref, f32[128,128]{1,0:T(8,128)S(1)} %shard_map.127.mine_ref, f32[128,128]{1,0:T(8,128)S(1)} %collective-permute-done.6.other_ref, s32[16,128]{1,0:T(8,128)S(1)} %bitcast.55, f32[128,128]{1,0:T(8,128)S(1)} %get-tuple-element.43.top_ref, ...), custom_call_target="tpu_custom_call" | custom-call | tf_op jit(solution)/shard_map/pallas_call | solution.py:660
  (19 shorter events, 0.0 us)
Async XLA Ops:
  0.6 13.0 %copy-start.3 = (bf16[8,32,128]{2,1,0:T(8,128)(2,1)S(1)}, bf16[8,32,128]{2,1,0:T(8,128)(2,1)}, u32[]{:S(2)}) copy-start(bf16[8,32,128]{2,1,0:T(8,128)(2,1)} %flux_ref.1) | copy-start | bytes 196612
  5.3 12.4 %copy-start.6 = (f32[56,128]{1,0:T(8,128)}, f32[56,128]{1,0:T(8,128)S(1)}, u32[]{:S(2)}) copy-start(f32[56,128]{1,0:T(8,128)S(1)} %get-tuple-element.28.own_hbm) | copy-start | bytes 86020
  5.3 12.5 %collective-permute-start = (f32[2,384,128]{2,1,0:T(8,128)S(1)}, f32[2,384,128]{2,1,0:T(8,128)S(1)}, u32[]{:S(2)}, u32[]{:S(2)}) collective-permute-start(f32[2,384,128]{2,1,0:T(8,128)S(1)} %get-tuple-element.26), channel_id=1, source_target_pairs={{0,8},{8,0},{16,24},{24,16},{32,40},{40,32},{48,56},{56,48},{1,9},... | collective-permute-start | bytes 1179656 | tf_op jit(solution)/shard_map/ppermute | solution.py:563
  5.4 12.4 %collective-permute-start.1 = (f32[2,384,128]{2,1,0:T(8,128)S(1)}, f32[2,384,128]{2,1,0:T(8,128)S(1)}, u32[]{:S(2)}, u32[]{:S(2)}) collective-permute-start(f32[2,384,128]{2,1,0:T(8,128)S(1)} %get-tuple-element.27), channel_id=1, source_target_pairs={{8,16},{16,8},{24,32},{32,24},{40,48},{48,40},{56,0},{0,56},{9,17}... | collective-permute-start | bytes 1179656 | tf_op jit(solution)/shard_map/ppermute | solution.py:563
  9.6 8.1 %collective-permute-start.3 = (f32[56,128]{1,0:T(8,128)S(1)}, f32[56,128]{1,0:T(8,128)S(1)}, u32[]{:S(2)}, u32[]{:S(2)}) collective-permute-start(f32[56,128]{1,0:T(8,128)S(1)} %get-tuple-element.28.own_hbm), channel_id=1, source_target_pairs={{1,2},{2,1},{3,4},{4,3},{5,6},{6,5},{7,0},{0,7},{9,10},{10,9},{11,... | collective-permute-start | bytes 86024 | tf_op jit(solution)/shard_map/ppermute | solution.py:563
  13.6 4.2 %collective-permute-start.2 = (f32[56,128]{1,0:T(8,128)S(1)}, f32[56,128]{1,0:T(8,128)S(1)}, u32[]{:S(2)}, u32[]{:S(2)}) collective-permute-start(f32[56,128]{1,0:T(8,128)S(1)} %get-tuple-element.28.own_hbm), channel_id=1, source_target_pairs={{0,1},{1,0},{2,3},{3,2},{4,5},{5,4},{6,7},{7,6},{8,9},{9,8},{10,11... | collective-permute-start | bytes 86024 | tf_op jit(solution)/shard_map/ppermute | solution.py:563
  17.7 6.2 %copy-start.9 = (f32[56,128]{1,0:T(8,128)}, f32[56,128]{1,0:T(8,128)S(1)}, u32[]{:S(2)}) copy-start(f32[56,128]{1,0:T(8,128)S(1)} %collective-permute-done.3.ewb_hbm) | copy-start | bytes 86020
  17.8 6.1 %copy-start.10 = (f32[56,128]{1,0:T(8,128)}, f32[56,128]{1,0:T(8,128)S(1)}, u32[]{:S(2)}) copy-start(f32[56,128]{1,0:T(8,128)S(1)} %collective-permute-done.2.ewa_hbm) | copy-start | bytes 86020
  17.8 6.1 %copy-start.7 = (f32[2,384,128]{2,1,0:T(8,128)}, f32[2,384,128]{2,1,0:T(8,128)S(1)}, u32[]{:S(2)}) copy-start(f32[2,384,128]{2,1,0:T(8,128)S(1)} %collective-permute-done.nsa_hbm) | copy-start | bytes 1179652
  17.8 6.1 %copy-start.8 = (f32[2,384,128]{2,1,0:T(8,128)}, f32[2,384,128]{2,1,0:T(8,128)S(1)}, u32[]{:S(2)}) copy-start(f32[2,384,128]{2,1,0:T(8,128)S(1)} %collective-permute-done.1.nsb_hbm) | copy-start | bytes 1179652
  17.8 27.1 %all-to-all-start = ((f32[64,32,128]{2,1,0:T(8,128)}), f32[64,32,128]{2,1,0:T(8,128)S(1)}, u32[]{:S(2)}, u32[]{:S(2)}) async-start(f32[64,32,128]{2,1,0:T(8,128)} %bitcast.21), calls=%async_computation | async-start | bytes 2097152 | tf_op jit(solution)/shard_map/all_to_all | solution.py:610
  23.9 17.1 %copy-start = (s32[8,512,4]{1,2,0:T(4,128)S(1)}, s32[8,512,4]{1,2,0:T(4,128)}, u32[]{:S(2)}) copy-start(s32[8,512,4]{1,2,0:T(4,128)} %param.20) | copy-start | bytes 196612
  24.0 17.0 %copy-start.4 = (s32[8,512,4]{1,2,0:T(4,128)S(1)}, s32[8,512,4]{1,2,0:T(4,128)}, u32[]{:S(2)}) copy-start(s32[8,512,4]{1,2,0:T(4,128)} %param.21) | copy-start | bytes 196612
  24.0 18.3 %copy-start.1 = (f32[8,62,62]{2,0,1:T(8,128)S(1)}, f32[8,62,62]{2,0,1:T(8,128)}, u32[]{:S(2)}) copy-start(f32[8,62,62]{2,0,1:T(8,128)} %param.17) | copy-start | bytes 369028
  24.0 18.3 %copy-start.5 = (s32[8,256]{1,0:T(8,128)S(1)}, s32[8,256]{1,0:T(8,128)}, u32[]{:S(2)}) copy-start(s32[8,256]{1,0:T(8,128)} %param.16) | copy-start | bytes 24580
  34.2 14.2 %collective-permute-start.7 = (f32[2,248,128]{2,1,0:T(8,128)}, f32[2,248,128]{2,1,0:T(8,128)S(1)}, u32[]{:S(2)}, u32[]{:S(2)}) collective-permute-start(f32[2,248,128]{2,1,0:T(8,128)} %get-tuple-element.39), channel_id=1, source_target_pairs={{0,8},{8,0},{16,24},{24,16},{32,40},{40,32},{48,56},{56,48},{1,9},... | collective-permute-start | bytes 761864 | tf_op jit(solution)/shard_map/ppermute | solution.py:563
  34.3 14.1 %collective-permute-start.8 = (f32[2,248,128]{2,1,0:T(8,128)}, f32[2,248,128]{2,1,0:T(8,128)S(1)}, u32[]{:S(2)}, u32[]{:S(2)}) collective-permute-start(f32[2,248,128]{2,1,0:T(8,128)} %get-tuple-element.40), channel_id=1, source_target_pairs={{8,16},{16,8},{24,32},{32,24},{40,48},{48,40},{56,0},{0,56},{9,17}... | collective-permute-start | bytes 761864 | tf_op jit(solution)/shard_map/ppermute | solution.py:563
  37.4 6.1 %collective-permute-start.5 = (f32[32,128]{1,0:T(8,128)}, f32[32,128]{1,0:T(8,128)S(1)}, u32[]{:S(2)}, u32[]{:S(2)}) collective-permute-start(f32[32,128]{1,0:T(8,128)} %get-tuple-element.34), channel_id=1, source_target_pairs={{1,2},{2,1},{3,4},{4,3},{5,6},{6,5},{7,0},{0,7},{9,10},{10,9},{11,... | collective-permute-start | bytes 49160 | tf_op jit(solution)/shard_map/ppermute | solution.py:563
  41.0 3.9 %collective-permute-start.4 = (f32[32,128]{1,0:T(8,128)}, f32[32,128]{1,0:T(8,128)S(1)}, u32[]{:S(2)}, u32[]{:S(2)}) collective-permute-start(f32[32,128]{1,0:T(8,128)} %get-tuple-element.34), channel_id=1, source_target_pairs={{0,1},{1,0},{2,3},{3,2},{4,5},{5,4},{6,7},{7,6},{8,9},{9,8},{10,11... | collective-permute-start | bytes 49160 | tf_op jit(solution)/shard_map/ppermute | solution.py:563
  45.7 11.1 %collective-permute-start.6 = (f32[128,128]{1,0:T(8,128)S(1)}, f32[128,128]{1,0:T(8,128)S(1)}, u32[]{:S(2)}, u32[]{:S(2)}) collective-permute-start(f32[128,128]{1,0:T(8,128)S(1)} %shard_map.127.mine_ref), channel_id=1, source_target_pairs={{0,64},{64,0},{1,65},{65,1},{2,66},{66,2},{3,67},{67,3},{4,68},{68... | collective-permute-start | bytes 196616 | tf_op jit(solution)/shard_map/ppermute | solution.py:563
  48.4 8.4 %copy-start.2 = (s32[8,256]{1,0:T(8,128)S(1)}, s32[8,256]{1,0:T(8,128)}, u32[]{:S(2)}) copy-start(s32[8,256]{1,0:T(8,128)} %param.15) | copy-start | bytes 24580
where the time goes:
time: 59.4 us; the launch traced here: 59.1 us
  Pallas kernels  31.8 us (54%)
  starting transfers between devices  23.9 us (40%)
  waiting for transfers between devices  1.83 us (3%)
  between operations  0.9 us (2%)
  other arithmetic  0.65 us (1%)
    ppermute x9, starting transfers between devices, swap(): return lax.ppermute(x, axis, pairs)  17.8 us
    pallas_call x1, Pallas kernels, per_device(): call(step_one_kernel, (shape(*tr.shape), shape(5 * levels * 16, 128), sha...  10.2 us
    pallas_call x1, Pallas kernels, per_device(): call(step_two_kernel, (shape(*tr.shape), shape(32 * count, 128)), [SM, HB...  8.36 us
    all_to_all x1, starting transfers between devices, per_device(): lax.all_to_all(blocks.reshape(pools, 4 * fluxes, 128), ('oy', 'ox'), spli...  6.08 us
    pallas_call x1, Pallas kernels, per_device(): call(remap_kernel, shape(pools * 4, fluxes, 128), [SM, VM, HB], [pltpu.VM...  4.13 us
    pallas_call x1, Pallas kernels, per_device(): call(pack_kernel, (shape(2, rows, 128), shape(2, rows, 128), shape(edge,...  4.01 us
    pallas_call x1, Pallas kernels, per_device(): call(finish_kernel, (shape(*tr.shape), shape(fluxes * 16, 128)), [SM] + [...  2.28 us
    ppermute x9, waiting for transfers between devices, swap(): return lax.ppermute(x, axis, pairs)  1.83 us
  transfers between devices with their start and end apart: 10, of which 2 were waited for; matrix products, arithmetic and copies ran while one was open for 0% of the time, Pallas kernels for 43%

commit v1 on v0

--- a/solution.py
+++ b/solution.py
@@ -14,7 +14,18 @@
 OY, OX, SEC, N_OY = 0, 1, 2, 3
 UNROLL_ONE = 4
 UNROLL_TWO = True
-UNROLL_MIX = 4
+UNROLL_MIX = 16
+
+
+class Place:
+    def __getitem__(self, entry):
+        if entry == N_OY:
+            return jnp.int32(lax.axis_size("oy"))
+        return lax.axis_index(("oy", "ox", "sec")[entry])
+
+
+def located(body):
+    return lambda *refs: body(Place(), *refs)
 
 
 def call(body, outs, in_specs, scratch=(), out_specs=None, limit=4):
@@ -570,8 +581,6 @@
     count, levels, lats, lons = tracers.shape
     n_oy, n_ox = lax.axis_size("oy"), lax.axis_size("ox")
     pools = n_oy * n_ox
-    oy, ox, sec = lax.axis_index("oy"), lax.axis_index("ox"), lax.axis_index("sec")
-    sc = jnp.stack([oy, ox, sec, jnp.int32(n_oy)]).astype(jnp.int32)
     fluxes, atm_rows, cells = atmos_fluxes.shape
     dests = dest_tiles.shape[2]
     classes = mix_matrices.shape[0]
@@ -580,17 +589,17 @@
     )
     land, kinds = to_tiles(land_sea), to_tiles(mix_class)
 
-    tr, u, v, k, land_hbm, sc = (in_place(x) for x in (tr, u, v, k, land, sc))
+    tr, u, v, k, land_hbm = (in_place(x) for x in (tr, u, v, k, land))
     dest_t = dest_tiles.transpose(0, 2, 1)
     offset_t = dest_offsets.transpose(0, 2, 1)
     rows = count * levels + 136
     edge = 8 * (count + 3)
     nsa, nsb, ew, slots = call(
-        pack_kernel,
+        located(pack_kernel),
         (shape(2, rows, 128), shape(2, rows, 128), shape(edge, 128), shape(dests, 128, dtype=jnp.int32)),
-        [SM] + [HB] * 6,
+        [HB] * 6,
         field_scratch(tr, u) + [pltpu.VMEM((dests, 128), jnp.int32), pltpu.SemaphoreType.DMA], limit=8,
-    )(sc, tr, u, v, k, land_hbm, in_place(dest_t))
+    )(tr, u, v, k, land_hbm, in_place(dest_t))
     nsa_in, nsb_in = swap(nsa, "oy", 0), swap(nsb, "oy", 1)
     ewa_in, ewb_in = swap(ew, "ox", 0), swap(ew, "ox", 1)
 
@@ -611,7 +620,7 @@
         blocks.reshape(pools, 4 * fluxes, 128), ("oy", "ox"), split_axis=0, concat_axis=0, tiled=True
     )
 
-    onehot = call(table_kernel, shape(16, pools * 4), [SM, VM, VM])(sc, dest_t, offset_t)
+    onehot = call(located(table_kernel), shape(16, pools * 4), [VM, VM])(dest_t, offset_t)
     lhs, units = call(
         prepare_kernel,
         (shape(64 * classes, 192, dtype=BF16), shape(2 * levels * 16, 128)),
@@ -620,12 +629,12 @@
     )(mix_matrices.transpose(1, 0, 2), kinds)
 
     moved, coef, nsa, nsb, ew = call(
-        step_one_kernel,
+        located(step_one_kernel),
         (
             shape(*tr.shape), shape(5 * levels * 16, 128),
             shape(2, count * levels, 128), shape(2, count * levels, 128), shape(8 * count, 128),
         ),
-        [SM] + [HB] * 10,
+        [HB] * 10,
         [pltpu.VMEM((2, rows, 128), F32), pltpu.VMEM((2, rows, 128), F32), pltpu.VMEM((4, 2, 64, 128), F32)]
         + field_scratch(tr, u)
         + [pltpu.VMEM((2, rows, 128), F32)] * 2
@@ -636,7 +645,7 @@
         ],
         [HB, HB, VM, VM, VM],
         60,
-    )(sc, tr, u, v, k, land_hbm, *(in_place(x) for x in (nsa_in, nsb_in, ewa_in, ewb_in, ew)))
+    )(tr, u, v, k, land_hbm, *(in_place(x) for x in (nsa_in, nsb_in, ewa_in, ewb_in, ew)))
     nsa_in, nsb_in = swap(nsa, "oy", 0), swap(nsb, "oy", 1)
     ewa_in, ewb_in = swap(ew, "ox", 0), swap(ew, "ox", 1)
 
@@ -645,21 +654,21 @@
         onehot, routed.reshape(pools * 4 * fluxes, 128), lhs
     )
     pre, top = call(
-        step_two_kernel,
+        located(step_two_kernel),
         (shape(*tr.shape), shape(32 * count, 128)),
-        [SM, HB, HB] + [VM] * 6,
+        [HB, HB] + [VM] * 6,
         [
             pltpu.VMEM((2, count * levels, 128), F32), pltpu.VMEM((2, count * levels, 128), F32),
             pltpu.VMEM((count * 1024, 128), F32), pltpu.VMEM(tr.shape, F32),
             pltpu.VMEM(coef.shape, F32), pltpu.SemaphoreType.DMA((10,)),
         ],
         limit=12,
-    )(sc, in_place(moved), in_place(coef), nsa_in, nsb_in, ewa_in, ewb_in, lhs, kinds)
+    )(in_place(moved), in_place(coef), nsa_in, nsb_in, ewa_in, ewb_in, lhs, kinds)
 
     other = swap(mine, "sec", 0)
     out, surface = call(
-        finish_kernel, (shape(*tr.shape), shape(fluxes * 16, 128)), [SM] + [VM] * 6
-    )(sc, mine, other, land, top, units, pre)
+        located(finish_kernel), (shape(*tr.shape), shape(fluxes * 16, 128)), [VM] * 6
+    )(mine, other, land, top, units, pre)
     return from_tiles(out, tracers.shape), from_tiles(surface, (fluxes, lats, lons))
 
 

time: 59.4 us -> 55.3 us (0.931)
  Pallas kernels: 31.8 us -> 27.5 us
  waiting for transfers between devices: 1.83 us -> 2.5 us
  other arithmetic: 0.65 us -> 0 us
    pallas_call x5, Pallas kernels: 26.1 us -> 21.8 us  [the longest x1 9.44 us: per_device(): call(located(step_one_kernel), (shape(*tr.shape), shape(5 * levels * 16,...]
    ppermute x9, waiting for transfers between devices: 1.83 us -> 2.49 us  [swap(): return lax.ppermute(x, axis, pairs)]
    another operation x1 -> x0, other arithmetic: 0.65 us -> none  [per_device(): sc = jnp.stack([oy, ox, sec, jnp.int32(n_oy)]).astype(jnp.int32)]
  transfers between devices with their start and end apart: 10 -> 10, of which waited for: 2 -> 2; matrix products, arithmetic and copies ran while one was open for 0% -> 0% of each run, Pallas kernels for 43% -> 41%
where the time goes in v1:
time: 55.3 us; the launch traced here: 55 us
  Pallas kernels  27.5 us (50%)
  starting transfers between devices  24.1 us (44%)
  waiting for transfers between devices  2.5 us (5%)
  between operations  0.89 us (2%)
    ppermute x9, starting transfers between devices, swap(): return lax.ppermute(x, axis, pairs)  18 us
    pallas_call x1, Pallas kernels, per_device(): call(located(step_one_kernel), (shape(*tr.shape), shape(5 * levels * 16,...  9.44 us
    pallas_call x1, Pallas kernels, per_device(): call(located(step_two_kernel), (shape(*tr.shape), shape(32 * count, 128))...  6.78 us
    all_to_all x1, starting transfers between devices, per_device(): lax.all_to_all(blocks.reshape(pools, 4 * fluxes, 128), ('oy', 'ox'), spli...  6.08 us
    pallas_call x1, Pallas kernels, per_device(): call(remap_kernel, shape(pools * 4, fluxes, 128), [SM, VM, HB], [pltpu.VM...  4.13 us
    pallas_call x1, Pallas kernels, per_device(): call(located(pack_kernel), (shape(2, rows, 128), shape(2, rows, 128), sha...  3.38 us
    ppermute x9, waiting for transfers between devices, swap(): return lax.ppermute(x, axis, pairs)  2.49 us
    pallas_call x1, Pallas kernels, per_device(): call(located(finish_kernel), (shape(*tr.shape), shape(fluxes * 16, 128)),...  1.64 us
  transfers between devices with their start and end apart: 10, of which 2 were waited for; matrix products, arithmetic and copies ran while one was open for 0% of the time, Pallas kernels for 41%

profile of v1, /device:TPU:0, one launch (start us, length us, event | category | flops | bytes accessed | tf_op | source)
XLA Modules:
  0.0 55.0 jit_solution(9043108974868958349)
XLA Ops:
  0.6 3.4 %shard_map.123 = (f32[2,384,128]{2,1,0:T(8,128)S(1)}, f32[2,384,128]{2,1,0:T(8,128)S(1)}, f32[56,128]{1,0:T(8,128)S(1)}, s32[4,128]{1,0:T(4,128)S(1)}) custom-call(f32[3968,128]{1,0:T(8,128)} %bitcast.56, f32[992,128]{1,0:T(8,128)} %bitcast.59, f32[992,128]{1,0:T(8,128)} %bitcast.61, f32[992,128]{1,0:T(8,128)} %bitcast.63, s32[16,128]{1,0:T(8,128)} %bitcast.50, ...), custom_call_target="tpu_custom_call" | custom-call | tf_op jit(solution)/shard_map/pallas_call | solution.py:597
  4.0 0.1 collective-permute-start
  4.1 4.2 %collective-permute-start.1 = (f32[2,384,128]{2,1,0:T(8,128)S(1)}, f32[2,384,128]{2,1,0:T(8,128)S(1)}, u32[]{:S(2)}, u32[]{:S(2)}) collective-permute-start(f32[2,384,128]{2,1,0:T(8,128)S(1)} %get-tuple-element.27), channel_id=1, source_target_pairs={{8,16},{16,8},{24,32},{32,24},{40,48},{48,40},{56,0},{0,56},{9,17}... | collective-permute-start | bytes 1179656 | tf_op jit(solution)/shard_map/ppermute | solution.py:574
  8.4 3.9 %collective-permute-start.3 = (f32[56,128]{1,0:T(8,128)S(1)}, f32[56,128]{1,0:T(8,128)S(1)}, u32[]{:S(2)}, u32[]{:S(2)}) collective-permute-start(f32[56,128]{1,0:T(8,128)S(1)} %get-tuple-element.28.refs_9_), channel_id=1, source_target_pairs={{1,2},{2,1},{3,4},{4,3},{5,6},{6,5},{7,0},{0,7},{9,10},{10,9},{11,... | collective-permute-start | bytes 86024 | tf_op jit(solution)/shard_map/ppermute | solution.py:574
  12.3 0.0 collective-permute-start.2
  12.3 4.1 %shard_map.124 = f32[256,8,128]{2,1,0:T(8,128)} custom-call(s32[4,128]{1,0:T(4,128)S(1)} %get-tuple-element.25.slot_ref, bf16[8,32,128]{2,1,0:T(8,128)(2,1)S(1)} %copy-done.3, bf16[32,4,128,128]{3,2,1,0:T(8,128)(2,1)} %bitcast.58), custom_call_target="tpu_custom_call" | custom-call | tf_op jit(solution)/shard_map/pallas_call | solution.py:606
  16.5 0.0 collective-permute-done.3.refs_8_
  16.5 0.0 collective-permute-done.2.refs_7_
  16.5 0.0 copy-start.10
  16.5 0.0 collective-permute-done.refs_5_
  16.5 0.0 collective-permute-done.1.refs_6_
  16.5 6.1 %all-to-all-start = ((f32[64,32,128]{2,1,0:T(8,128)}), f32[64,32,128]{2,1,0:T(8,128)S(1)}, u32[]{:S(2)}, u32[]{:S(2)}) async-start(f32[64,32,128]{2,1,0:T(8,128)} %bitcast.18), calls=%async_computation | async-start | bytes 2097152 | tf_op jit(solution)/shard_map/all_to_all | solution.py:619
  22.7 0.0 copy-start
  22.7 0.0 copy-start.4
  22.7 0.0 copy-start.1
  22.7 0.0 copy-start.5
  22.7 9.4 %shard_map.125 = (f32[3968,128]{1,0:T(8,128)}, f32[4960,128]{1,0:T(8,128)}, f32[2,248,128]{2,1,0:T(8,128)}, f32[2,248,128]{2,1,0:T(8,128)}, f32[32,128]{1,0:T(8,128)}) custom-call(f32[3968,128]{1,0:T(8,128)} %bitcast.57, f32[992,128]{1,0:T(8,128)} %bitcast.60, f32[992,128]{1,0:T(8,128)} %bitcast.62, f32[992,128]{1,0:T(8,128)} %bitcast.64, ...), custom_call_target="tpu_custom_call" | custom-call | tf_op jit(solution)/shard_map/pallas_call | solution.py:631
  32.2 0.1 collective-permute-start.7
  32.3 3.0 %collective-permute-start.8 = (f32[2,248,128]{2,1,0:T(8,128)}, f32[2,248,128]{2,1,0:T(8,128)S(1)}, u32[]{:S(2)}, u32[]{:S(2)}) collective-permute-start(f32[2,248,128]{2,1,0:T(8,128)} %get-tuple-element.40), channel_id=1, source_target_pairs={{8,16},{16,8},{24,32},{32,24},{40,48},{48,40},{56,0},{0,56},{9,17}... | collective-permute-start | bytes 761864 | tf_op jit(solution)/shard_map/ppermute | solution.py:574
  35.3 3.6 %collective-permute-start.5 = (f32[32,128]{1,0:T(8,128)}, f32[32,128]{1,0:T(8,128)S(1)}, u32[]{:S(2)}, u32[]{:S(2)}) collective-permute-start(f32[32,128]{1,0:T(8,128)} %get-tuple-element.34), channel_id=1, source_target_pairs={{1,2},{2,1},{3,4},{4,3},{5,6},{6,5},{7,0},{0,7},{9,10},{10,9},{11,... | collective-permute-start | bytes 49160 | tf_op jit(solution)/shard_map/ppermute | solution.py:574
  39.0 0.0 collective-permute-start.4
  39.0 0.6 %shard_map.122.onehot_ref = f32[16,256]{1,0:T(8,128)S(1)} custom-call(s32[8,4,512]{2,1,0:T(4,128)S(1)} %bitcast.48, s32[8,4,512]{2,1,0:T(4,128)S(1)} %bitcast.53), custom_call_target="tpu_custom_call" | custom-call | tf_op jit(solution)/shard_map/pallas_call | solution.py:623
  39.6 0.8 %shard_map.126 = (bf16[512,192]{1,0:T(8,128)(2,1)S(1)}, f32[1984,128]{1,0:T(8,128)S(1)}) custom-call(f32[62,8,62]{2,1,0:T(8,128)S(1)} %bitcast.49, s32[16,128]{1,0:T(8,128)S(1)} %bitcast.54), custom_call_target="tpu_custom_call" | custom-call | tf_op jit(solution)/shard_map/pallas_call | solution.py:624
  40.4 1.0 %collective-permute-done.5.refs_5_ = f32[32,128]{1,0:T(8,128)S(1)} collective-permute-done((f32[32,128]{1,0:T(8,128)}, f32[32,128]{1,0:T(8,128)S(1)}, u32[]{:S(2)}, u32[]{:S(2)}) %collective-permute-start.5) | collective-permute-done | bytes 16416 | tf_op jit(solution)/shard_map/ppermute | solution.py:574
  41.4 1.5 %collective-permute-done.4.refs_4_ = f32[32,128]{1,0:T(8,128)S(1)} collective-permute-done((f32[32,128]{1,0:T(8,128)}, f32[32,128]{1,0:T(8,128)S(1)}, u32[]{:S(2)}, u32[]{:S(2)}) %collective-permute-start.4) | collective-permute-done | bytes 16416 | tf_op jit(solution)/shard_map/ppermute | solution.py:574
  42.9 0.0 all-to-all-done
  42.9 0.7 %shard_map.127.refs_0_ = f32[128,128]{1,0:T(8,128)S(1)} custom-call(f32[16,256]{1,0:T(8,128)S(1)} %shard_map.122.onehot_ref, f32[2048,128]{1,0:T(8,128)S(1)} %bitcast.46, bf16[512,192]{1,0:T(8,128)(2,1)S(1)} %get-tuple-element.36.after_ref.refs_6_), custom_call_target="tpu_custom_call" | custom-call | tf_op jit(solution)/shard_map/pallas_call | solution.py:653
  43.7 2.9 %collective-permute-start.6 = (f32[128,128]{1,0:T(8,128)S(1)}, f32[128,128]{1,0:T(8,128)S(1)}, u32[]{:S(2)}, u32[]{:S(2)}) collective-permute-start(f32[128,128]{1,0:T(8,128)S(1)} %shard_map.127.refs_0_), channel_id=1, source_target_pairs={{0,64},{64,0},{1,65},{65,1},{2,66},{66,2},{3,67},{67,3},{4,68},{68... | collective-permute-start | bytes 196616 | tf_op jit(solution)/shard_map/ppermute | solution.py:574
  46.6 0.0 collective-permute-done.7.refs_2_
  46.6 0.0 collective-permute-done.8.refs_3_
  46.6 6.8 %shard_map.128 = (f32[3968,128]{1,0:T(8,128)S(1)}, f32[128,128]{1,0:T(8,128)S(1)}) custom-call(f32[3968,128]{1,0:T(8,128)} %get-tuple-element.37.refs_0_, f32[4960,128]{1,0:T(8,128)} %get-tuple-element.38.refs_1_, f32[2,248,128]{2,1,0:T(8,128)S(1)} %collective-permute-done.7.refs_2_, f32[2,248,128]{2,1,0:T(8,128)S(1)} %collective-permute-done.8.refs_3_, ...), custom_call_target="tpu_custom_call" | custom-call | tf_op jit(solution)/shard_map/pallas_call | solution.py:656
  53.4 1.6 %shard_map.129 = (f32[3968,128]{1,0:T(8,128)}, f32[128,128]{1,0:T(8,128)}) custom-call(f32[128,128]{1,0:T(8,128)S(1)} %shard_map.127.refs_0_, f32[128,128]{1,0:T(8,128)S(1)} %collective-permute-done.6.refs_1_, s32[16,128]{1,0:T(8,128)S(1)} %bitcast.52, f32[128,128]{1,0:T(8,128)S(1)} %get-tuple-element.43.refs_3_, f32[1984,128]{1,0:T(8,128)S(1)} %get-tuple-element.44.refs_4_, ...), custom_call_target="tpu_custom_call" | custom-call | tf_op jit(solution)/shard_map/pallas_call | solution.py:669
  (18 shorter events, 0.0 us)
Async XLA Ops:
  0.6 11.7 %copy-start.3 = (bf16[8,32,128]{2,1,0:T(8,128)(2,1)S(1)}, bf16[8,32,128]{2,1,0:T(8,128)(2,1)}, u32[]{:S(2)}) copy-start(bf16[8,32,128]{2,1,0:T(8,128)(2,1)} %flux_ref.1) | copy-start | bytes 196612
  4.0 12.4 %copy-start.6 = (f32[56,128]{1,0:T(8,128)}, f32[56,128]{1,0:T(8,128)S(1)}, u32[]{:S(2)}) copy-start(f32[56,128]{1,0:T(8,128)S(1)} %get-tuple-element.28.refs_9_) | copy-start | bytes 86020
  4.0 12.5 %collective-permute-start = (f32[2,384,128]{2,1,0:T(8,128)S(1)}, f32[2,384,128]{2,1,0:T(8,128)S(1)}, u32[]{:S(2)}, u32[]{:S(2)}) collective-permute-start(f32[2,384,128]{2,1,0:T(8,128)S(1)} %get-tuple-element.26), channel_id=1, source_target_pairs={{0,8},{8,0},{16,24},{24,16},{32,40},{40,32},{48,56},{56,48},{1,9},... | collective-permute-start | bytes 1179656 | tf_op jit(solution)/shard_map/ppermute | solution.py:574
  4.1 12.4 %collective-permute-start.1 = (f32[2,384,128]{2,1,0:T(8,128)S(1)}, f32[2,384,128]{2,1,0:T(8,128)S(1)}, u32[]{:S(2)}, u32[]{:S(2)}) collective-permute-start(f32[2,384,128]{2,1,0:T(8,128)S(1)} %get-tuple-element.27), channel_id=1, source_target_pairs={{8,16},{16,8},{24,32},{32,24},{40,48},{48,40},{56,0},{0,56},{9,17}... | collective-permute-start | bytes 1179656 | tf_op jit(solution)/shard_map/ppermute | solution.py:574
  8.4 8.1 %collective-permute-start.3 = (f32[56,128]{1,0:T(8,128)S(1)}, f32[56,128]{1,0:T(8,128)S(1)}, u32[]{:S(2)}, u32[]{:S(2)}) collective-permute-start(f32[56,128]{1,0:T(8,128)S(1)} %get-tuple-element.28.refs_9_), channel_id=1, source_target_pairs={{1,2},{2,1},{3,4},{4,3},{5,6},{6,5},{7,0},{0,7},{9,10},{10,9},{11,... | collective-permute-start | bytes 86024 | tf_op jit(solution)/shard_map/ppermute | solution.py:574
  12.3 4.2 %collective-permute-start.2 = (f32[56,128]{1,0:T(8,128)S(1)}, f32[56,128]{1,0:T(8,128)S(1)}, u32[]{:S(2)}, u32[]{:S(2)}) collective-permute-start(f32[56,128]{1,0:T(8,128)S(1)} %get-tuple-element.28.refs_9_), channel_id=1, source_target_pairs={{0,1},{1,0},{2,3},{3,2},{4,5},{5,4},{6,7},{7,6},{8,9},{9,8},{10,11... | collective-permute-start | bytes 86024 | tf_op jit(solution)/shard_map/ppermute | solution.py:574
  16.5 6.2 %copy-start.9 = (f32[56,128]{1,0:T(8,128)}, f32[56,128]{1,0:T(8,128)S(1)}, u32[]{:S(2)}) copy-start(f32[56,128]{1,0:T(8,128)S(1)} %collective-permute-done.3.refs_8_) | copy-start | bytes 86020
  16.5 6.1 %copy-start.10 = (f32[56,128]{1,0:T(8,128)}, f32[56,128]{1,0:T(8,128)S(1)}, u32[]{:S(2)}) copy-start(f32[56,128]{1,0:T(8,128)S(1)} %collective-permute-done.2.refs_7_) | copy-start | bytes 86020
  16.5 6.1 %copy-start.7 = (f32[2,384,128]{2,1,0:T(8,128)}, f32[2,384,128]{2,1,0:T(8,128)S(1)}, u32[]{:S(2)}) copy-start(f32[2,384,128]{2,1,0:T(8,128)S(1)} %collective-permute-done.refs_5_) | copy-start | bytes 1179652
  16.5 6.1 %copy-start.8 = (f32[2,384,128]{2,1,0:T(8,128)}, f32[2,384,128]{2,1,0:T(8,128)S(1)}, u32[]{:S(2)}) copy-start(f32[2,384,128]{2,1,0:T(8,128)S(1)} %collective-permute-done.1.refs_6_) | copy-start | bytes 1179652
  16.5 26.4 %all-to-all-start = ((f32[64,32,128]{2,1,0:T(8,128)}), f32[64,32,128]{2,1,0:T(8,128)S(1)}, u32[]{:S(2)}, u32[]{:S(2)}) async-start(f32[64,32,128]{2,1,0:T(8,128)} %bitcast.18), calls=%async_computation | async-start | bytes 2097152 | tf_op jit(solution)/shard_map/all_to_all | solution.py:619
  22.7 16.3 %copy-start = (s32[8,512,4]{1,2,0:T(4,128)S(1)}, s32[8,512,4]{1,2,0:T(4,128)}, u32[]{:S(2)}) copy-start(s32[8,512,4]{1,2,0:T(4,128)} %param.20) | copy-start | bytes 196612
  22.7 16.3 %copy-start.4 = (s32[8,512,4]{1,2,0:T(4,128)S(1)}, s32[8,512,4]{1,2,0:T(4,128)}, u32[]{:S(2)}) copy-start(s32[8,512,4]{1,2,0:T(4,128)} %param.21) | copy-start | bytes 196612
  22.7 16.9 %copy-start.1 = (f32[8,62,62]{2,0,1:T(8,128)S(1)}, f32[8,62,62]{2,0,1:T(8,128)}, u32[]{:S(2)}) copy-start(f32[8,62,62]{2,0,1:T(8,128)} %param.17) | copy-start | bytes 369028
  22.7 16.9 %copy-start.5 = (s32[8,256]{1,0:T(8,128)S(1)}, s32[8,256]{1,0:T(8,128)}, u32[]{:S(2)}) copy-start(s32[8,256]{1,0:T(8,128)} %param.16) | copy-start | bytes 24580
  32.2 14.4 %collective-permute-start.7 = (f32[2,248,128]{2,1,0:T(8,128)}, f32[2,248,128]{2,1,0:T(8,128)S(1)}, u32[]{:S(2)}, u32[]{:S(2)}) collective-permute-start(f32[2,248,128]{2,1,0:T(8,128)} %get-tuple-element.39), channel_id=1, source_target_pairs={{0,8},{8,0},{16,24},{24,16},{32,40},{40,32},{48,56},{56,48},{1,9},... | collective-permute-start | bytes 761864 | tf_op jit(solution)/shard_map/ppermute | solution.py:574
  32.3 14.3 %collective-permute-start.8 = (f32[2,248,128]{2,1,0:T(8,128)}, f32[2,248,128]{2,1,0:T(8,128)S(1)}, u32[]{:S(2)}, u32[]{:S(2)}) collective-permute-start(f32[2,248,128]{2,1,0:T(8,128)} %get-tuple-element.40), channel_id=1, source_target_pairs={{8,16},{16,8},{24,32},{32,24},{40,48},{48,40},{56,0},{0,56},{9,17}... | collective-permute-start | bytes 761864 | tf_op jit(solution)/shard_map/ppermute | solution.py:574
  35.3 6.1 %collective-permute-start.5 = (f32[32,128]{1,0:T(8,128)}, f32[32,128]{1,0:T(8,128)S(1)}, u32[]{:S(2)}, u32[]{:S(2)}) collective-permute-start(f32[32,128]{1,0:T(8,128)} %get-tuple-element.34), channel_id=1, source_target_pairs={{1,2},{2,1},{3,4},{4,3},{5,6},{6,5},{7,0},{0,7},{9,10},{10,9},{11,... | collective-permute-start | bytes 49160 | tf_op jit(solution)/shard_map/ppermute | solution.py:574
  39.0 3.9 %collective-permute-start.4 = (f32[32,128]{1,0:T(8,128)}, f32[32,128]{1,0:T(8,128)S(1)}, u32[]{:S(2)}, u32[]{:S(2)}) collective-permute-start(f32[32,128]{1,0:T(8,128)} %get-tuple-element.34), channel_id=1, source_target_pairs={{0,1},{1,0},{2,3},{3,2},{4,5},{5,4},{6,7},{7,6},{8,9},{9,8},{10,11... | collective-permute-start | bytes 49160 | tf_op jit(solution)/shard_map/ppermute | solution.py:574
  43.7 9.7 %collective-permute-start.6 = (f32[128,128]{1,0:T(8,128)S(1)}, f32[128,128]{1,0:T(8,128)S(1)}, u32[]{:S(2)}, u32[]{:S(2)}) collective-permute-start(f32[128,128]{1,0:T(8,128)S(1)} %shard_map.127.refs_0_), channel_id=1, source_target_pairs={{0,64},{64,0},{1,65},{65,1},{2,66},{66,2},{3,67},{67,3},{4,68},{68... | collective-permute-start | bytes 196616 | tf_op jit(solution)/shard_map/ppermute | solution.py:574
  46.6 6.8 %copy-start.2 = (s32[8,256]{1,0:T(8,128)S(1)}, s32[8,256]{1,0:T(8,128)}, u32[]{:S(2)}) copy-start(s32[8,256]{1,0:T(8,128)} %param.15) | copy-start | bytes 24580
